TPU v7x, 512 devices: a whole 4x8x8 slice. The times are simulated.
512 devices in a mesh: vocab: 32 (over x, z), dp: 16 (over y, core).
Axes of the slice: x: 4, y: 8, z: 8, core: 2. Of those that a mesh axis runs over, the one named last changes fastest.
Arguments:
- ex_hidden: bfloat16 [128, 7168], P('dp'), may hold values from -72 to 72
- ex_target: int32 [128], P('dp'), may hold values from 0 to 129279
- q_hidden: bfloat16 [128, 7168], P('dp'), may hold values from -72 to 72
- q_target: int32 [128], P('dp'), may hold values from 0 to 129279
- head: bfloat16 [129280, 7168], P('vocab', 'dp'), may hold values from -0.25 to 0.25
- out_proj: bfloat16 [129280, 64], P('vocab'), may hold values from -2 to 2
- in_proj: bfloat16 [7168, 64], P('vocab'), may hold values from -0.0234375 to 0.0234375
Outputs:
- scores: float32 [128, 128], P('dp')
All inputs are finite; a program needn't handle non-finite values.
Results may differ from a plain program's by a relative error of at most 0.0012.
Values may be sent and summed in bfloat16 or wider, within the bound.
A program may use at most 64 MiB of HBM per device.

v0:
```python
import jax
import jax.numpy as jnp
from jax import lax
from jax.sharding import PartitionSpec as P


def body(ex_hidden, ex_target, q_hidden, q_target, head, out_proj, in_proj):
    ex_rows = ex_hidden.shape[0]
    stacked = jnp.concatenate([ex_hidden, q_hidden], 0)
    targets = jnp.concatenate([ex_target, q_target], 0)
    own_rows = stacked.shape[0]
    vocab_width = head.shape[0]
    slice_width = in_proj.shape[0]
    spread = lax.all_to_all(stacked, "dp", split_axis=1, concat_axis=0, tiled=True)
    summed = lax.psum(
        lax.dot_general(spread, head, (((1,), (1,)), ((), ())), preferred_element_type=jnp.float32),
        "dp",
    )
    logits = lax.dynamic_slice_in_dim(summed, lax.axis_index("dp") * own_rows, own_rows, 0)
    local_max = jnp.max(logits, axis=1)
    row_top = lax.pmax(local_max, "vocab")
    shifted = jnp.exp(logits - row_top[:, None])
    row_sum = lax.psum(jnp.sum(shifted, axis=1), "vocab")
    prob = shifted / row_sum[:, None]
    offset = lax.axis_index("vocab") * vocab_width
    columns = lax.broadcasted_iota(jnp.int32, (1, vocab_width), 1) + offset
    onehot = (columns == targets[:, None]).astype(jnp.float32)
    resid = (prob - onehot).astype(jnp.bfloat16)
    a_part = jnp.dot(resid, out_proj, preferred_element_type=jnp.float32)
    features = lax.dynamic_slice_in_dim(
        stacked, lax.axis_index("vocab") * slice_width, slice_width, 1
    )
    b_part = jnp.dot(features, in_proj, preferred_element_type=jnp.float32)
    a_proj, b_proj = lax.psum((a_part, b_part), "vocab")
    query_a, query_b = (
        lax.all_gather(a_proj[ex_rows:], "dp", axis=0, tiled=True),
        lax.all_gather(b_proj[ex_rows:], "dp", axis=0, tiled=True),
    )
    left = jnp.dot(a_proj[:ex_rows], query_a.T, precision=lax.Precision.HIGHEST)
    right = jnp.dot(b_proj[:ex_rows], query_b.T, precision=lax.Precision.HIGHEST)
    return left * right


def solution(mesh):
    in_specs = (
        P("dp", None),
        P("dp"),
        P("dp", None),
        P("dp"),
        P("vocab", "dp"),
        P("vocab", None),
        P("vocab", None),
    )
    out_specs = P("dp", None)
    return jax.shard_map(body, mesh=mesh, in_specs=in_specs, out_specs=out_specs, check_vma=False)
```

profile of v0, /device:TPU:1, one launch (start us, length us, event | category | flops | bytes accessed | tf_op | source)
XLA Modules:
  0.0 489.6 jit_solution(2109032585652176225)
XLA Ops:
  6.5 0.0 copy-start
  6.5 0.0 all-reduce.3.cloned.1.call-start
  6.5 1.0 constant_dynamic-update-slice_fusion.1
  7.5 0.9 constant_dynamic-update-slice_fusion
  8.4 0.3 all_to_all.14
  8.7 0.2 copy.8
  8.9 21.2 %all_to_all.19 = bf16[16,16,448]{2,0,1:T(8,128)(2,1)S(1)} all-to-all(bf16[16,16,448]{2,0,1:T(8,128)(2,1)S(1)} %copy.8), channel_id=1, replica_groups=mesh['vocab'=32,'dp'=16] {'dp'}, dimensions={1} | all-to-all | bytes 458752 | tf_op jit(solution)/shard_map/all_to_all | solution.py:14
  30.0 5.3 %fusion.9 = f32[256,4040]{1,0:T(8,128)} fusion(bf16[256,448]{1,0:T(8,128)(2,1)S(1)} %bitcast.9, bf16[4040,448]{0,1:T(8,128)(2,1)} %param.11), kind=kOutput, calls=%fused_computation.17 | convolution fusion | flops 926679040 | bytes 7986176 | tf_op jit(solution)/shard_map/dot_general | solution.py:16
  35.4 0.0 copy-start.1
  35.4 0.0 copy-start.2
  35.4 0.0 copy-start.3
  35.4 0.0 all-reduce.3.cloned.1.call-update
  35.4 0.7 copy-done.1
  36.1 0.2 fusion.2
  36.3 124.1 %all-reduce.3.cloned.1.call-done = f32[256,4040]{1,0:T(8,128)} async-done(((f32[256,4040]{1,0:T(8,128)}), f32[256,4040]{1,0:T(8,128)}) %all-reduce.3.cloned.1.call-update) | async-done | bytes 4136976 | tf_op jit(solution)/shard_map/psum | solution.py:15
  160.4 1.1 dynamic-slice_reduce_fusion
  161.5 61.7 %pmax.7 = f32[16]{0:T(128)S(1)} all-reduce(f32[16]{0:T(128)S(1)} %dynamic-slice_reduce_fusion), channel_id=1, replica_groups=mesh['vocab'=32,'dp'=16] {'vocab'}, use_global_device_ids=true, to_apply=%region_2.0 | all-reduce | flops 16 | bytes 128 | tf_op jit(solution)/shard_map/pmax | solution.py:21
  223.1 1.2 fusion
  224.3 0.0 copy-done.2
  224.3 0.0 copy-done.3
  224.3 0.1 pad_add_fusion
  224.4 55.8 %psum.29 = f32[16]{0:T(128)S(1)} all-reduce(f32[16]{0:T(128)S(1)} %fusion), channel_id=1, replica_groups=mesh['vocab'=32,'dp'=16] {'vocab'}, use_global_device_ids=true, to_apply=%region_4.0 | all-reduce | flops 16 | bytes 128 | tf_op jit(solution)/shard_map/psum | solution.py:23
  280.2 0.0 copy-done
  280.2 1.3 fusion.1
  281.4 112.3 %all-reduce = (f32[16,64]{1,0:T(8,128)S(1)}, f32[16,64]{1,0:T(8,128)S(1)}) all-reduce(f32[16,64]{1,0:T(8,128)S(1)} %fusion.1, f32[16,64]{1,0:T(8,128)S(1)} %fusion.2), channel_id=1, replica_groups=mesh['vocab'=32,'dp'=16] {'vocab'}, use_global_device_ids=true, to_apply=%region_5.0 | all-reduce | flops 2048 | bytes 16384 | tf_op jit(solution)/shard_map/psum | solution.py:34
  393.7 70.8 %all_gather.7 = f32[128,64]{1,0:T(8,128)S(1)} all-gather(f32[8,64]{1,0:T(8,128)S(1)} %slice.19), channel_id=1, replica_groups=mesh['vocab'=32,'dp'=16] {'dp'}, dimensions={0}, use_global_device_ids=true | all-gather | bytes 34816 | tf_op jit(solution)/shard_map/all_gather | solution.py:37
  464.6 17.1 %all_gather.6 = f32[128,64]{1,0:T(8,128)S(1)} all-gather(f32[8,64]{1,0:T(8,128)S(1)} %slice.17), channel_id=1, replica_groups=mesh['vocab'=32,'dp'=16] {'dp'}, dimensions={0}, use_global_device_ids=true | all-gather | bytes 34816 | tf_op jit(solution)/shard_map/all_gather | solution.py:36
  481.7 0.2 fusion.5
  481.9 0.9 convolution_multiply_fusion
  (3 shorter events, 0.0 us)
Async XLA Ops:
  6.5 273.7 %copy-start = (bf16[4040,64]{0,1:T(8,128)(2,1)S(1)}, bf16[4040,64]{0,1:T(8,128)(2,1)}, u32[]{:S(2)}) copy-start(bf16[4040,64]{0,1:T(8,128)(2,1)} %param.12) | copy-start | bytes 1551364
  6.5 153.8 %all-reduce.3.cloned.1.call-start = ((), (), s32[]{:S(2)}) async-start(), calls=%async_computation.1 | async-start | bytes 8388608 | tf_op jit(solution)/shard_map/psum | solution.py:15
  35.4 0.8 copy-start.1
  35.4 189.0 %copy-start.2 = (s32[8]{0:T(128)S(1)}, s32[8]{0:T(128)}, u32[]{:S(2)}) copy-start(s32[8]{0:T(128)} %param.10) | copy-start | bytes 100
  35.4 189.0 %copy-start.3 = (s32[8]{0:T(128)S(1)}, s32[8]{0:T(128)}, u32[]{:S(2)}) copy-start(s32[8]{0:T(128)} %param.8) | copy-start | bytes 100
Sparse Core Ops, SparseCore 0:
  35.5 124.8 all-reduce.2
where the time goes:
time: 490 us
  blocking collectives  339 us (69%)
  waiting for transfers between devices  124 us (25%)
  between operations  13.4 us (3%)
  matrix products  7.8 us (2%)
    psum x1, waiting for transfers between devices, body(): lax.psum(lax.dot_general(spread, head, (((1,), (1,)), ((), ())), preferre...  124 us
    psum x1, blocking collectives, body(): a_proj, b_proj = lax.psum((a_part, b_part), 'vocab')  112 us
    all_gather x1, blocking collectives, body(): lax.all_gather(b_proj[ex_rows:], 'dp', axis=0, tiled=True)  70.8 us
    pmax x1, blocking collectives, body(): row_top = lax.pmax(local_max, 'vocab')  61.7 us
    psum x1, blocking collectives, body(): row_sum = lax.psum(jnp.sum(shifted, axis=1), 'vocab')  55.8 us
    all_to_all x1, blocking collectives, body(): lax.all_to_all(stacked, 'dp', split_axis=1, concat_axis=0, tiled=True)  21.2 us
    all_gather x1, blocking collectives, body(): lax.all_gather(a_proj[ex_rows:], 'dp', axis=0, tiled=True)  17.1 us
  transfers between devices with their start and end apart: 1, of which 1 were waited for; matrix products, arithmetic and copies ran while one was open for 0% of the time, Pallas kernels for 0%

commit v1 on v0

v1 whole, which is shorter than its diff:
```python
import functools

import jax
import jax.numpy as jnp
from jax import lax
from jax.experimental import pallas as pl
from jax.experimental.pallas import tpu as pltpu
from jax.sharding import PartitionSpec as P

MESH = pl.DeviceIdType.MESH
NT = (((1,), (1,)), ((), ()))
CHIPS = 8
CORES = 2
NX, NZ = 4, 8
ROWS = 8
VOCAB = 4040
PAD = 4096
COLS = 448
KP = 64
TILE = 512
HALVES = 2
HALF = PAD // HALVES
F32 = jnp.float32
BF16 = jnp.bfloat16


def kernel(
    ex_hbm, ext_hbm, q_hbm, qt_hbm, head_hbm, out_hbm, in_hbm,
    scores_ref,
    ex_v, q_v, head_v, outp_v, inp_v, ext_s, qt_s,
    xs, xbuf, pbuf, sbuf, obuf, rbuf, wz,
    early_own, early_z, early_x, late_own, late_z, late_x, late_mid, early_mid,
    qbuf,
    load_sem, a2a_send, a2a_recv, sib_send, sib_recv, ring_send, ring_recv,
    ez_send, ez_recv, ex_send, ex_recv, lz_send, lz_recv, lx_send, lx_recv, q_send, q_recv,
):
    dp = lax.axis_index("dp")
    voc = lax.axis_index("vocab")
    y, core = dp // CORES, dp % CORES
    x, z = voc // NZ, voc % NZ
    sib = 1 - core

    def dp_of(chip, c):
        return lax.rem(chip + 2 * CHIPS, CHIPS) * CORES + c

    dp_partners = [dp_of(y + rc, c) for rc in range(CHIPS) for c in (core, sib)][1:]
    z_partners = [x * NZ + lax.rem(z + r, NZ) for r in range(1, NZ)]
    x_partners = [lax.rem(x + r, NX) * NZ + z for r in range(1, NX)]

    barrier = pltpu.get_barrier_semaphore()
    for d in dp_partners:
        pl.semaphore_signal(barrier, inc=1, device_id={"dp": d}, device_id_type=MESH)
    for d in z_partners + x_partners:
        pl.semaphore_signal(barrier, inc=1, device_id={"vocab": d}, device_id_type=MESH)

    loads = [
        pltpu.make_async_copy(src, dst, load_sem.at[i])
        for i, (src, dst) in enumerate(
            [(ex_hbm, ex_v), (q_hbm, q_v), (head_hbm, head_v), (ext_hbm, ext_s), (qt_hbm, qt_s), (out_hbm, outp_v), (in_hbm, inp_v)]
        )
    ]
    for c in loads:
        c.start()
    sends = []

    def push(src, dst, ssem, rsem, target):
        c = pltpu.make_async_remote_copy(
            src_ref=src, dst_ref=dst, send_sem=ssem, recv_sem=rsem, device_id=target, device_id_type=MESH
        )
        c.start()
        sends.append(c)
        return c

    loads[0].wait()
    loads[1].wait()
    for j in range(CHIPS * CORES):
        cut = pl.ds(COLS * j, COLS)
        block = jnp.concatenate([ex_v[:, cut].astype(F32), q_v[:, cut].astype(F32)], 0)
        xs[j] = block.astype(BF16)
    xbuf[0, 0] = xs[dp]

    pl.semaphore_wait(barrier, len(dp_partners) + len(z_partners) + len(x_partners))

    a2a = {}
    for rc in (1, 7, 2, 6, 3, 5, 4, 0):
        for k, c in enumerate((core, sib)):
            if rc == 0 and k == 0:
                continue
            t = dp_of(y + rc, c)
            a2a[rc, k] = push(
                xs.at[t], xbuf.at[rc, k], a2a_send.at[rc * 2 + k], a2a_recv.at[rc * 2 + k], {"dp": t}
            )

    for i in (3, 4, 5, 6):
        loads[i].wait()
    row = lax.broadcasted_iota(jnp.int32, (2 * ROWS, 1), 0)
    tcol = jnp.zeros((2 * ROWS, 1), jnp.int32)
    for r in range(ROWS):
        tcol = jnp.where(row == r, ext_s[r], tcol)
        tcol = jnp.where(row == ROWS + r, qt_s[r], tcol)
    tcol = tcol - voc * VOCAB
    hot = (lax.broadcasted_iota(jnp.int32, (2 * ROWS, VOCAB), 1) == tcol).astype(F32).astype(BF16)
    t_part = jnp.dot(hot, outp_v[...], preferred_element_type=F32)
    wz[...] = jnp.zeros_like(wz)
    depth = inp_v.shape[0]
    wz[pl.ds(pl.multiple_of(depth * lax.rem(voc, 2), 16), depth), :] = inp_v[...]
    b_part = jnp.dot(xs[voc // 2], wz[...], preferred_element_type=F32)
    early_own[...] = jnp.concatenate([t_part, b_part], 1)
    ez = [
        push(early_own, early_z.at[r], ez_send.at[r], ez_recv.at[r], {"vocab": t}) for r, t in enumerate(z_partners)
    ]

    loads[2].wait()

    def logits(rcs):
        for rc in rcs:
            for k in range(2):
                if (rc, k) in a2a:
                    a2a[rc, k].wait_recv()
        rows = jnp.concatenate([xbuf[rc, k] for rc in rcs for k in range(2)], 0)
        for n in range(0, PAD, TILE):
            width = min(TILE, VOCAB - n)
            part = lax.dot_general(rows, head_v[n:n + width, :], NT, preferred_element_type=F32)
            i = 0
            for rc in rcs:
                for k in range(2):
                    pbuf[rc, k, :, n:n + width] = part[i:i + 2 * ROWS]
                    i += 2 * ROWS
        for rc in rcs:
            for k in range(2):
                pbuf[rc, k, :, VOCAB:PAD] = jnp.zeros((2 * ROWS, PAD - VOCAB), F32)
            twin[rc] = push(
                pbuf.at[rc, 1], sbuf.at[rc], sib_send.at[rc], sib_recv.at[rc], {"dp": dp_of(y, sib)}
            )

    twin = {}
    waited = set()
    ring = {}

    def chip_sum(direction, rc, half):
        rows = pl.ds(ROWS * direction, ROWS)
        lanes = pl.ds(HALF * half, HALF)
        if rc not in waited:
            twin[rc].wait_recv()
            waited.add(rc)
        return pbuf[rc, 0, rows, lanes] + sbuf[rc, rows, lanes]

    def ring_step(s):
        for half in range(HALVES):
            lanes = pl.ds(HALF * half, HALF)
            for direction in range(2):
                rc = 1 + s if direction == 0 else 7 - s
                total = chip_sum(direction, rc, half)
                if s:
                    ring[direction, s - 1, half].wait_recv()
                    total = total + rbuf[direction, s - 1, :, lanes]
                obuf[direction, s, :, lanes] = total
                i = (direction * 7 + s) * HALVES + half
                to = dp_of(y + 1, core) if direction == 0 else dp_of(y - 1, core)
                ring[direction, s, half] = push(
                    obuf.at[direction, s, :, lanes], rbuf.at[direction, s, :, lanes],
                    ring_send.at[i], ring_recv.at[i], {"dp": to},
                )

    logits((1, 7))
    ring_step(0)
    logits((2, 6))
    ring_step(1)
    logits((3, 5))
    ring_step(2)
    logits((4, 0))
    ring_step(3)

    for c in ez:
        c.wait_recv()
    mid = early_own[...]
    for r in range(NZ - 1):
        mid = mid + early_z[r]
    early_mid[...] = mid
    exs = [
        push(early_mid, early_x.at[r], ex_send.at[r], ex_recv.at[r], {"vocab": t}) for r, t in enumerate(x_partners)
    ]
    ring_step(4)
    ring_step(5)
    for c in exs:
        c.wait_recv()
    for r in range(NX - 1):
        mid = mid + early_x[r]
    ring_step(6)

    own = []
    for half in range(HALVES):
        for direction in range(2):
            ring[direction, 6, half].wait_recv()
    for direction in range(2):
        rows = pl.ds(ROWS * direction, ROWS)
        own.append(pbuf[0, 0, rows, :VOCAB] + (sbuf_wait(twin, waited, sbuf, rows)) + rbuf[direction, 6, :, :VOCAB])
    full = jnp.concatenate(own, 0)
    top = jnp.max(full, axis=1, keepdims=True)
    e = jnp.exp(full - top)
    mass = jnp.sum(e, axis=1, keepdims=True)
    hi = e.astype(BF16)
    lo = (e - hi.astype(F32)).astype(BF16)
    num = jnp.dot(jnp.concatenate([hi, lo], 0), outp_v[...], preferred_element_type=F32)
    num = num[:2 * ROWS] + num[2 * ROWS:]
    quarter = (2 * ROWS, KP // 2)
    late_own[...] = jnp.concatenate([num, jnp.broadcast_to(top, quarter), jnp.broadcast_to(mass, quarter)], 1)

    lane = lax.broadcasted_iota(jnp.int32, (2 * ROWS, 2 * KP), 1)
    is_top = (lane >= KP) & (lane < KP + KP // 2)

    def merge(parts):
        tops = [p[:, KP:KP + 1] for p in parts]
        best = functools.reduce(jnp.maximum, tops)
        total = sum(p * jnp.exp(t - best) for p, t in zip(parts, tops))
        return jnp.where(is_top, best, total)

    lz = [push(late_own, late_z.at[r], lz_send.at[r], lz_recv.at[r], {"vocab": t}) for r, t in enumerate(z_partners)]
    for c in lz:
        c.wait_recv()
    merged = merge([late_own[...]] + [late_z[r] for r in range(NZ - 1)])
    late_mid[...] = merged
    lx = [push(late_mid, late_x.at[r], lx_send.at[r], lx_recv.at[r], {"vocab": t}) for r, t in enumerate(x_partners)]
    for c in lx:
        c.wait_recv()
    merged = merge([merged] + [late_x[r] for r in range(NX - 1)])
    a_proj = merged[:, :KP] / merged[:, 2 * KP - 1:] - mid[:, :KP]
    factors = jnp.concatenate([a_proj, mid[:, KP:]], 1)
    qbuf[dp] = factors[ROWS:]
    qs = []
    for r in range(1, CHIPS * CORES):
        qs.append(push(qbuf.at[dp], qbuf.at[dp], q_send.at[r], q_recv.at[r], {"dp": lax.rem(dp + r, CHIPS * CORES)}))
    mine = factors[:ROWS]
    zero = jnp.zeros((ROWS, KP), F32)
    both = jnp.concatenate(
        [jnp.concatenate([mine[:, :KP], zero], 1), jnp.concatenate([zero, mine[:, KP:]], 1)], 0
    )
    for c in qs:
        c.wait_recv()
    queries = qbuf[...].reshape(CHIPS * CORES * ROWS, 2 * KP)
    inner = lax.dot_general(both, queries, NT, precision=lax.Precision.HIGHEST, preferred_element_type=F32)
    scores_ref[...] = inner[:ROWS] * inner[ROWS:]
    for c in sends:
        c.wait_send()


def sbuf_wait(twin, waited, sbuf, rows):
    if 0 not in waited:
        twin[0].wait_recv()
        waited.add(0)
    return sbuf[0, rows, :VOCAB]


def body(ex_hidden, ex_target, q_hidden, q_target, head, out_proj, in_proj):
    dma = pltpu.SemaphoreType.DMA
    vm = pltpu.VMEM
    two = 2 * ROWS
    scratch = [
        vm(ex_hidden.shape, BF16), vm(q_hidden.shape, BF16), vm(head.shape, BF16), vm(out_proj.shape, BF16),
        vm(in_proj.shape, BF16), pltpu.SMEM((ROWS,), jnp.int32), pltpu.SMEM((ROWS,), jnp.int32),
        vm((CHIPS * CORES, two, COLS), BF16), vm((CHIPS, 2, two, COLS), BF16),
        vm((CHIPS, 2, two, PAD), F32), vm((CHIPS, two, PAD), F32),
        vm((2, CHIPS - 1, ROWS, PAD), F32), vm((2, CHIPS - 1, ROWS, PAD), F32), vm((COLS, KP), BF16),
        vm((two, 2 * KP), F32), vm((NZ - 1, two, 2 * KP), F32), vm((NX - 1, two, 2 * KP), F32),
        vm((two, 2 * KP), F32), vm((NZ - 1, two, 2 * KP), F32), vm((NX - 1, two, 2 * KP), F32),
        vm((two, 2 * KP), F32), vm((two, 2 * KP), F32),
        vm((CHIPS * CORES, ROWS, 2 * KP), F32),
        dma((7,)), dma((16,)), dma((16,)), dma((8,)), dma((8,)), dma((14 * HALVES,)), dma((14 * HALVES,)),
        dma((7,)), dma((7,)), dma((3,)), dma((3,)), dma((7,)), dma((7,)), dma((3,)), dma((3,)), dma((16,)), dma((16,)),
    ]
    return pl.pallas_call(
        kernel,
        out_shape=jax.ShapeDtypeStruct((ROWS, CHIPS * CORES * ROWS), F32),
        in_specs=[pl.BlockSpec(memory_space=pl.ANY)] * 7,
        out_specs=pl.BlockSpec(memory_space=pltpu.VMEM),
        scratch_shapes=scratch,
        compiler_params=pltpu.CompilerParams(
            collective_id=0, has_side_effects=True, vmem_limit_bytes=40 * 1024 * 1024
        ),
    )(ex_hidden, ex_target, q_hidden, q_target, head, out_proj, in_proj)


def solution(mesh):
    in_specs = (
        P("dp", None),
        P("dp"),
        P("dp", None),
        P("dp"),
        P("vocab", "dp"),
        P("vocab", None),
        P("vocab", None),
    )
    return jax.shard_map(body, mesh=mesh, in_specs=in_specs, out_specs=P("dp", None), check_vma=False)
```

time: 490 us -> 78.8 us (0.16)
  blocking collectives: 339 us -> 0 us
  waiting for transfers between devices: 124 us -> 0 us
  Pallas kernels: 0 us -> 66.7 us
  between operations: 13.4 us -> 0.06 us
  local copies, waits for them, and re-layouts: 3.07 us -> 11.7 us
  matrix products: 7.8 us -> 0 us
    psum x2 -> x0, blocking collectives: 168 us -> none  [the longest x1 112 us: body(): a_proj, b_proj = lax.psum((a_part, b_part), 'vocab')]
    psum x1 -> x0, waiting for transfers between devices: 124 us -> none  [body(): lax.psum(lax.dot_general(spread, head, (((1,), (1,)), ((), ())), preferre...]
    all_gather x2 -> x0, blocking collectives: 88 us -> none  [the longest x1 70.8 us: body(): lax.all_gather(b_proj[ex_rows:], 'dp', axis=0, tiled=True)]
    pallas_call x0 -> x1, Pallas kernels: none -> 66.7 us  [body(): pl.pallas_call(kernel, out_shape=jax.ShapeDtypeStruct((ROWS, CHIPS * CORE...]
    pmax x1 -> x0, blocking collectives: 61.7 us -> none  [body(): row_top = lax.pmax(local_max, 'vocab')]
    all_to_all x1 -> x0, blocking collectives: 21.2 us -> none  [body(): lax.all_to_all(stacked, 'dp', split_axis=1, concat_axis=0, tiled=True)]
    unnamed x9 -> x14, local copies, waits for them, and re-layouts: 1.7 us -> 11.7 us
    dot_general x5 -> x0, matrix products: 7.8 us -> none  [the longest x1 5.31 us: body(): lax.dot_general(spread, head, (((1,), (1,)), ((), ())), preferred_element...]
  transfers between devices with their start and end apart: 1 -> 0, of which waited for: 1 -> 0; matrix products, arithmetic and copies ran while one was open for 0% -> 0% of each run, Pallas kernels for 0% -> 0%
where the time goes in v1:
time: 78.8 us; the launch traced here: 78.5 us
  Pallas kernels  66.7 us (85%)
  local copies, waits for them, and re-layouts  11.7 us (15%)
    pallas_call x1, Pallas kernels, body(): pl.pallas_call(kernel, out_shape=jax.ShapeDtypeStruct((ROWS, CHIPS * CORE...  66.7 us
    unnamed x14, local copies, waits for them, and re-layouts  11.7 us

profile of v1, /device:TPU:1, one launch (start us, length us, event | category | flops | bytes accessed | tf_op | source)
XLA Modules:
  0.0 78.5 jit_solution(7414391263357264055)
XLA Ops:
  0.0 0.9 %copy.10.in_hbm = bf16[224,64]{1,0:T(8,128)(2,1)S(1)} copy(bf16[224,64]{0,1:T(8,128)(2,1)} %param.13) | data formatting | bytes 57344 | tf_op args[6]
  0.9 1.5 %copy.9.out_hbm = bf16[4040,64]{1,0:T(8,128)(2,1)S(1)} copy(bf16[4040,64]{0,1:T(8,128)(2,1)} %param.12) | data formatting | bytes 1034240 | tf_op args[5]
  2.4 0.0 copy-start.1
  2.4 0.0 copy-start.2
  2.4 0.0 copy-start.3
  2.4 0.0 copy-start.4
  2.5 6.5 %copy.8.head_hbm = bf16[4040,448]{1,0:T(8,128)(2,1)} copy(bf16[4040,448]{0,1:T(8,128)(2,1)} %param.11) | data formatting | bytes 7239680 | tf_op args[4]
  9.0 0.0 copy-done.1
  9.0 0.0 copy-done.2
  9.0 0.0 copy-done.3
  9.0 0.0 copy-done.4
  9.0 0.0 copy-start
  9.0 2.2 %copy-done = bf16[4040,448]{1,0:T(8,128)(2,1)S(1)} copy-done((bf16[4040,448]{1,0:T(8,128)(2,1)S(1)}, bf16[4040,448]{1,0:T(8,128)(2,1)}, u32[]{:S(2)}) %copy-start) | copy-done | bytes 3619864
  11.2 66.7 %shard_map.73 = f32[8,128]{1,0:T(8,128)S(1)} custom-call(bf16[8,7168]{1,0:T(8,128)(2,1)S(1)} %copy-done.1, s32[8]{0:T(128)S(1)} %copy-done.3, bf16[8,7168]{1,0:T(8,128)(2,1)S(1)} %copy-done.2, s32[8]{0:T(128)S(1)} %copy-done.4, bf16[4040,448]{1,0:T(8,128)(2,1)S(1)} %copy-done, bf16[4040,64]{1,0:T(8,128)(2,1)S(1)} %copy.9.out_hbm, ...), custom_call_target="tpu_custom_call" | custom-call | tf_op jit(solution)/shard_map/pallas_call | solution.py:271
  77.9 0.6 copy.12
Async XLA Ops:
  2.4 6.5 %copy-start.1 = (bf16[8,7168]{1,0:T(8,128)(2,1)S(1)}, bf16[8,7168]{1,0:T(8,128)(2,1)}, u32[]{:S(2)}) copy-start(bf16[8,7168]{1,0:T(8,128)(2,1)} %ex_hbm.1) | copy-start | bytes 344068
  2.4 6.5 %copy-start.2 = (bf16[8,7168]{1,0:T(8,128)(2,1)S(1)}, bf16[8,7168]{1,0:T(8,128)(2,1)}, u32[]{:S(2)}) copy-start(bf16[8,7168]{1,0:T(8,128)(2,1)} %q_hbm.1) | copy-start | bytes 344068
  2.4 6.5 %copy-start.3 = (s32[8]{0:T(128)S(1)}, s32[8]{0:T(128)}, u32[]{:S(2)}) copy-start(s32[8]{0:T(128)} %ext_hbm.1) | copy-start | bytes 100
  2.4 6.5 %copy-start.4 = (s32[8]{0:T(128)S(1)}, s32[8]{0:T(128)}, u32[]{:S(2)}) copy-start(s32[8]{0:T(128)} %qt_hbm.1) | copy-start | bytes 100
  9.0 2.2 %copy-start = (bf16[4040,448]{1,0:T(8,128)(2,1)S(1)}, bf16[4040,448]{1,0:T(8,128)(2,1)}, u32[]{:S(2)}) copy-start(bf16[4040,448]{1,0:T(8,128)(2,1)} %copy.8.head_hbm) | copy-start | bytes 10859524
